TPU v7x, 1024 devices: a whole 8x8x8 slice. The times are simulated.
1024 devices in a mesh: gx: 16 (over y, core), gy: 64 (over x, z).
Axes of the slice: x: 8, y: 8, z: 8, core: 2. Of those that a mesh axis runs over, the one named last changes fastest.
Arguments:
- kelvin_deviation: float32 [256, 4096, 128], P('gx', 'gy'), may hold values from -5 to 5
- vapour_content: float32 [256, 4096, 128], P('gx', 'gy'), may hold values from 0.05 to 0.5
- murky_sky_marker: int32 [256, 4096], P('gx', 'gy'), may hold values 0 or 1
- beam_incidence_ratio: bfloat16 [256, 4096], P('gx', 'gy'), may hold values from 0.099609375 to 1
- illuminated_profile_slots: int32 [16, 64, 1024], P('gx', 'gy'), may hold values from 0 to 1023, as said below
- illuminated_prefix_tally: int32 [16, 64], P('gx', 'gy'), may hold values from 0 to 1024, as said below
- uptake_coefficients: float32 [128, 128], replicated, may hold values from 0.002 to 0.2
- insolation_by_gpoint: float32 [128], replicated, may hold values from 0.02 to 0.1
Outputs:
- kelvin_after_step: float32 [256, 4096, 128], P('gx', 'gy')
- shortwave_gain_rate: float32 [256, 4096, 128], P('gx', 'gy')
Inputs may be any that keep to these rules, and one draw needn't show every extreme that they name: `illuminated_profile_slots`: each device's entries are a permutation of its 1024 local column indices. `illuminated_prefix_tally`: each count is a multiple of 16; a device's count plus that of the device 8 away along gx (half the gx cycle) is at most 1024.
All inputs are finite; a program needn't handle non-finite values. No bound on the sum of `murky_sky_marker` on one device may be relied on, other than what follows from the above.
Results may differ from a plain program's by a relative error of at most 0.0027.
Values may be sent and summed in bfloat16 or wider, within the bound.
A program may use at most 32 MiB of HBM per device.

v0:
```python
import math

import jax
import jax.numpy as jnp
from jax import lax
from jax.sharding import PartitionSpec as P


def extended(shard, sides, width):
    for axis, dim in sides:
        devices, length = (lax.axis_size(axis), shard.shape[dim])
        up = [(i, (i + 1) % devices) for i in range(devices)]
        down = [(j, i) for i, j in up]
        last = lax.slice_in_dim(shard, length - width, length, axis=dim)
        leading = lax.slice_in_dim(shard, 0, width, axis=dim)
        before = lax.ppermute(last, axis, up)
        after = lax.ppermute(leading, axis, down)
        shard = jnp.concatenate([before, shard, after], axis=dim)
    return shard


def profile_ingredients(kelvin_deviation, vapour_content, murky_sky_marker):
    murky_scaling = 1.0 + 3.0 * murky_sky_marker.astype(jnp.float32)[..., None]
    return (vapour_content * murky_scaling * jnp.exp(0.25 * kelvin_deviation)).astype(jnp.bfloat16)


def radiate(retained_heat_gain, cosine, uptake_coefficients, insolation_by_gpoint):
    column_total, layer_tally = retained_heat_gain.shape
    triangle = (
        lax.broadcasted_iota(jnp.int32, (layer_tally, layer_tally), 0)
        <= lax.broadcasted_iota(jnp.int32, (layer_tally, layer_tally), 1)
    ).astype(jnp.float32)
    tile_rows = math.gcd(column_total, 32)

    def tile_flux(pair):
        rows_here, cos_here = pair
        weighted = rows_here.astype(jnp.float32)[:, :, None] * uptake_coefficients[None, :, :]
        depth = jnp.einsum("tmg,ml->tlg", weighted, triangle, precision=lax.Precision.HIGHEST)
        return jnp.dot(
            jnp.exp(-depth / cos_here[:, None, None]),
            insolation_by_gpoint,
            precision=lax.Precision.HIGHEST,
        )

    fluxes = lax.map(
        tile_flux,
        (
            retained_heat_gain.reshape(column_total // tile_rows, tile_rows, layer_tally),
            cosine.reshape(column_total // tile_rows, tile_rows),
        ),
    ).reshape(column_total, layer_tally)
    incoming = jnp.broadcast_to(jnp.sum(insolation_by_gpoint), (column_total, 1))
    overhead = jnp.concatenate([incoming, fluxes[:, :-1]], axis=1)
    return cosine[:, None] * (overhead - fluxes)


def local(
    kelvin_deviation,
    vapour_content,
    murky_sky_marker,
    beam_incidence_ratio,
    illuminated_profile_slots,
    illuminated_prefix_tally,
    uptake_coefficients,
    insolation_by_gpoint,
):
    westerly_span_size, southerly_span_size, layer_tally = kelvin_deviation.shape
    column_grid = westerly_span_size * southerly_span_size
    cycle_size = lax.axis_size("gx")
    retained_heat_gain = profile_ingredients(
        kelvin_deviation, vapour_content, murky_sky_marker
    ).reshape(column_grid, layer_tally)
    cosine = beam_incidence_ratio.reshape(column_grid)
    listing = illuminated_profile_slots.reshape(column_grid)
    lit_total = illuminated_prefix_tally.reshape(())
    ranks = jnp.argsort(listing)
    listed_absorb = retained_heat_gain[listing]
    listed_cos = cosine[listing]
    live_rows = jnp.arange(column_grid, dtype=jnp.int32) < lit_total
    slot_count = column_grid // cycle_size
    capacity = column_grid // 2
    send_cos = jnp.where(live_rows, listed_cos, jnp.zeros_like(listed_cos)).reshape(
        slot_count, cycle_size
    )
    got_absorb, got_cos = (
        lax.all_to_all(
            listed_absorb.reshape(slot_count, cycle_size, layer_tally),
            "gx",
            split_axis=1,
            concat_axis=1,
            tiled=True,
        ),
        lax.all_to_all(send_cos, "gx", split_axis=1, concat_axis=1, tiled=True),
    )
    flat_absorb = got_absorb.reshape(column_grid, layer_tally)
    flat_cos = got_cos.reshape(column_grid)
    filled = flat_cos > 0
    target = jnp.cumsum(filled.astype(jnp.int32)) - 1
    picked = (
        jnp.zeros((capacity,), jnp.int32)
        .at[jnp.where(filled, target, capacity)]
        .set(jnp.arange(column_grid, dtype=jnp.int32), mode="drop")
    )
    valid = jnp.arange(capacity, dtype=jnp.int32) < jnp.sum(filled.astype(jnp.int32))
    packed_cos = jnp.where(valid, flat_cos[picked].astype(jnp.float32), 1.0)
    heated = radiate(flat_absorb[picked], packed_cos, uptake_coefficients, insolation_by_gpoint)
    spread_back = jnp.where(filled[:, None], heated[jnp.maximum(target, 0)], 0.0).reshape(
        slot_count, cycle_size, layer_tally
    )
    listed_heat = lax.all_to_all(
        spread_back, "gx", split_axis=1, concat_axis=1, tiled=True
    ).reshape(column_grid, layer_tally)
    shortwave_gain_rate = listed_heat[ranks].reshape(
        westerly_span_size, southerly_span_size, layer_tally
    )
    margin_wrapped_map = extended(kelvin_deviation, (("gx", 0), ("gy", 1)), 1)
    adjacent_to_profile = (
        margin_wrapped_map[2:, 1:-1]
        + margin_wrapped_map[:-2, 1:-1]
        + margin_wrapped_map[1:-1, 2:]
        + margin_wrapped_map[1:-1, :-2]
    )
    kelvin_after_step = (
        kelvin_deviation
        + 0.2 * (adjacent_to_profile - 4.0 * kelvin_deviation)
        + shortwave_gain_rate
    )
    return (kelvin_after_step, shortwave_gain_rate)


def solution(mesh):
    in_specs = (
        P("gx", "gy", None),
        P("gx", "gy", None),
        P("gx", "gy"),
        P("gx", "gy"),
        P("gx", "gy", None),
        P("gx", "gy"),
        P(),
        P(),
    )
    out_specs = (P("gx", "gy", None), P("gx", "gy", None))
    return jax.shard_map(local, mesh=mesh, in_specs=in_specs, out_specs=out_specs, check_vma=False)
```

profile of v0, /device:TPU:1, one launch (start us, length us, event | category | flops | bytes accessed | tf_op | source)
XLA Modules:
  0.0 162.0 jit_solution(12113080603274420486)
XLA Ops:
  2.9 6.8 %gather_fusion = bf16[1024]{0:T(1024)(128)(2,1)S(1)} fusion(bf16[1024]{0:T(1024)(128)(2,1)S(1)} %reshape.216, s32[1024]{0:T(1024)S(1)} %broadcast_clamp_fusion.1), kind=kCustom, calls=%fused_computation | custom fusion | bytes 8192 | tf_op jit(solution)/shard_map/gather | solution.py:78
  10.5 17.4 %all-to-all-start = ((bf16[64,16,1]{0,2,1:T(2,128)(2,1)}), bf16[64,16,1]{0,2,1:T(2,128)(2,1)S(1)}, u32[]{:S(2)}, u32[]{:S(2)}) async-start(bf16[64,16,1]{0,2,1:T(2,128)(2,1)} %copy.10), calls=%async_computation | async-start | bytes 16384 | tf_op jit(solution)/shard_map/all_to_all | solution.py:93
  30.4 4.5 %all-to-all-done = bf16[64,16,1]{0,2,1:T(2,128)(2,1)S(1)} async-done(((bf16[64,16,1]{0,2,1:T(2,128)(2,1)}), bf16[64,16,1]{0,2,1:T(2,128)(2,1)S(1)}, u32[]{:S(2)}, u32[]{:S(2)}) %all-to-all-start) | async-done | bytes 2080 | tf_op jit(solution)/shard_map/all_to_all | solution.py:93
  36.4 4.3 %scatter_custom_fusion = s32[512]{0:T(512)S(1)} fusion(s32[1024]{0:T(1024)S(1)} %bitcast.72, s32[1024]{0:T(1024)S(1)} %iota.55, s32[]{:T(128)} %copy.32), kind=kCustom, calls=%fused_computation.63 | custom fusion | bytes 2052 | tf_op jit(solution)/shard_map/scatter | solution.py:102
  40.8 3.5 %gather_fusion.1 = bf16[512]{0:T(512)(128)(2,1)S(1)} fusion(bf16[1024]{0:T(1024)(128)(2,1)S(1)} %reshape.218, s32[1024]{0:T(1024)S(1)} %pad_clamp_fusion), kind=kCustom, calls=%fused_computation.1 | custom fusion | bytes 4096 | tf_op jit(solution)/shard_map/gather | solution.py:105
  44.6 3.2 %gather_fusion.2 = bf16[1024,128]{1,0:T(8,128)(2,1)S(1)} fusion(bf16[1024,128]{1,0:T(8,128)(2,1)S(1)} %bitcast.58, s32[1024]{0:T(1024)S(1)} %broadcast_clamp_fusion.1), kind=kCustom, calls=%fused_computation.2 | custom fusion | bytes 528384 | tf_op jit(solution)/shard_map/gather | solution.py:77
  48.6 4.0 %all-to-all-start.1 = ((bf16[64,16,128]{2,0,1:T(8,128)(2,1)}), bf16[64,16,128]{2,0,1:T(8,128)(2,1)S(1)}, u32[]{:S(2)}, u32[]{:S(2)}) async-start(bf16[64,16,128]{2,0,1:T(8,128)(2,1)} %copy.14), calls=%async_computation.1 | async-start | bytes 524288 | tf_op jit(solution)/shard_map/all_to_all | solution.py:86
  53.9 10.5 %all-to-all-done.1 = bf16[64,16,128]{2,0,1:T(8,128)(2,1)S(1)} async-done(((bf16[64,16,128]{2,0,1:T(8,128)(2,1)}), bf16[64,16,128]{2,0,1:T(8,128)(2,1)S(1)}, u32[]{:S(2)}, u32[]{:S(2)}) %all-to-all-start.1) | async-done | bytes 262176 | tf_op jit(solution)/shard_map/all_to_all | solution.py:86
  66.0 54.2 %while.11 = (s32[]{:T(128)}, f32[16,32,128]{2,1,0:T(8,128)S(1)}, bf16[16,32,128]{2,1,0:T(8,128)(2,1)S(1)}, f32[128,128]{0,1:T(8,128)S(1)}, f32[16,32]{1,0:T(8,128)S(1)}, /*index=5*/f32[128]{0:T(128)S(1)}, s32[]{:T(128)}) while((s32[]{:T(128)}, f32[16,32,128]{2,1,0:T(8,128)S(1)}, bf16[16,32,128]{2,1,0:T(8,128)(2,1)S(1)}, ...), condition=%wide.region_5.6_spmd.clone, body=%wide.region_4.5_spmd.clone.sunk | while | flops 813207552 | bytes 4350945 | solution.py:45
  66.0 1.8 %fusion.42 = f32[32,128,128]{2,1,0:T(8,128)S(1)} fusion(f32[128,128]{0,1:T(8,128)S(1)} %get-tuple-element.138, f32[32,128]{1,0:T(8,128)S(1)} %bitcast_convert_fusion.2), kind=kOutput, calls=%fused_computation.13.clone.1 | convolution fusion | flops 805863424 | bytes 2179072 | tf_op jit(solution)/shard_map/while/body/eval_jaxpr/tmg,ml->tlg/dot_general | solution.py:38
  69.4 1.8 %fusion.42 = f32[32,128,128]{2,1,0:T(8,128)S(1)} fusion(f32[128,128]{0,1:T(8,128)S(1)} %get-tuple-element.138, f32[32,128]{1,0:T(8,128)S(1)} %bitcast_convert_fusion.2), kind=kOutput, calls=%fused_computation.13.clone.1 | convolution fusion | flops 805863424 | bytes 2179072 | tf_op jit(solution)/shard_map/while/body/eval_jaxpr/tmg,ml->tlg/dot_general | solution.py:38
  72.8 1.8 %fusion.42 = f32[32,128,128]{2,1,0:T(8,128)S(1)} fusion(f32[128,128]{0,1:T(8,128)S(1)} %get-tuple-element.138, f32[32,128]{1,0:T(8,128)S(1)} %bitcast_convert_fusion.2), kind=kOutput, calls=%fused_computation.13.clone.1 | convolution fusion | flops 805863424 | bytes 2179072 | tf_op jit(solution)/shard_map/while/body/eval_jaxpr/tmg,ml->tlg/dot_general | solution.py:38
  76.2 1.8 %fusion.42 = f32[32,128,128]{2,1,0:T(8,128)S(1)} fusion(f32[128,128]{0,1:T(8,128)S(1)} %get-tuple-element.138, f32[32,128]{1,0:T(8,128)S(1)} %bitcast_convert_fusion.2), kind=kOutput, calls=%fused_computation.13.clone.1 | convolution fusion | flops 805863424 | bytes 2179072 | tf_op jit(solution)/shard_map/while/body/eval_jaxpr/tmg,ml->tlg/dot_general | solution.py:38
  79.6 1.8 %fusion.42 = f32[32,128,128]{2,1,0:T(8,128)S(1)} fusion(f32[128,128]{0,1:T(8,128)S(1)} %get-tuple-element.138, f32[32,128]{1,0:T(8,128)S(1)} %bitcast_convert_fusion.2), kind=kOutput, calls=%fused_computation.13.clone.1 | convolution fusion | flops 805863424 | bytes 2179072 | tf_op jit(solution)/shard_map/while/body/eval_jaxpr/tmg,ml->tlg/dot_general | solution.py:38
  83.0 1.8 %fusion.42 = f32[32,128,128]{2,1,0:T(8,128)S(1)} fusion(f32[128,128]{0,1:T(8,128)S(1)} %get-tuple-element.138, f32[32,128]{1,0:T(8,128)S(1)} %bitcast_convert_fusion.2), kind=kOutput, calls=%fused_computation.13.clone.1 | convolution fusion | flops 805863424 | bytes 2179072 | tf_op jit(solution)/shard_map/while/body/eval_jaxpr/tmg,ml->tlg/dot_general | solution.py:38
  86.4 1.8 %fusion.42 = f32[32,128,128]{2,1,0:T(8,128)S(1)} fusion(f32[128,128]{0,1:T(8,128)S(1)} %get-tuple-element.138, f32[32,128]{1,0:T(8,128)S(1)} %bitcast_convert_fusion.2), kind=kOutput, calls=%fused_computation.13.clone.1 | convolution fusion | flops 805863424 | bytes 2179072 | tf_op jit(solution)/shard_map/while/body/eval_jaxpr/tmg,ml->tlg/dot_general | solution.py:38
  89.7 1.8 %fusion.42 = f32[32,128,128]{2,1,0:T(8,128)S(1)} fusion(f32[128,128]{0,1:T(8,128)S(1)} %get-tuple-element.138, f32[32,128]{1,0:T(8,128)S(1)} %bitcast_convert_fusion.2), kind=kOutput, calls=%fused_computation.13.clone.1 | convolution fusion | flops 805863424 | bytes 2179072 | tf_op jit(solution)/shard_map/while/body/eval_jaxpr/tmg,ml->tlg/dot_general | solution.py:38
  93.1 1.8 %fusion.42 = f32[32,128,128]{2,1,0:T(8,128)S(1)} fusion(f32[128,128]{0,1:T(8,128)S(1)} %get-tuple-element.138, f32[32,128]{1,0:T(8,128)S(1)} %bitcast_convert_fusion.2), kind=kOutput, calls=%fused_computation.13.clone.1 | convolution fusion | flops 805863424 | bytes 2179072 | tf_op jit(solution)/shard_map/while/body/eval_jaxpr/tmg,ml->tlg/dot_general | solution.py:38
  96.5 1.8 %fusion.42 = f32[32,128,128]{2,1,0:T(8,128)S(1)} fusion(f32[128,128]{0,1:T(8,128)S(1)} %get-tuple-element.138, f32[32,128]{1,0:T(8,128)S(1)} %bitcast_convert_fusion.2), kind=kOutput, calls=%fused_computation.13.clone.1 | convolution fusion | flops 805863424 | bytes 2179072 | tf_op jit(solution)/shard_map/while/body/eval_jaxpr/tmg,ml->tlg/dot_general | solution.py:38
  99.9 1.8 %fusion.42 = f32[32,128,128]{2,1,0:T(8,128)S(1)} fusion(f32[128,128]{0,1:T(8,128)S(1)} %get-tuple-element.138, f32[32,128]{1,0:T(8,128)S(1)} %bitcast_convert_fusion.2), kind=kOutput, calls=%fused_computation.13.clone.1 | convolution fusion | flops 805863424 | bytes 2179072 | tf_op jit(solution)/shard_map/while/body/eval_jaxpr/tmg,ml->tlg/dot_general | solution.py:38
  103.3 1.8 %fusion.42 = f32[32,128,128]{2,1,0:T(8,128)S(1)} fusion(f32[128,128]{0,1:T(8,128)S(1)} %get-tuple-element.138, f32[32,128]{1,0:T(8,128)S(1)} %bitcast_convert_fusion.2), kind=kOutput, calls=%fused_computation.13.clone.1 | convolution fusion | flops 805863424 | bytes 2179072 | tf_op jit(solution)/shard_map/while/body/eval_jaxpr/tmg,ml->tlg/dot_general | solution.py:38
  106.7 1.8 %fusion.42 = f32[32,128,128]{2,1,0:T(8,128)S(1)} fusion(f32[128,128]{0,1:T(8,128)S(1)} %get-tuple-element.138, f32[32,128]{1,0:T(8,128)S(1)} %bitcast_convert_fusion.2), kind=kOutput, calls=%fused_computation.13.clone.1 | convolution fusion | flops 805863424 | bytes 2179072 | tf_op jit(solution)/shard_map/while/body/eval_jaxpr/tmg,ml->tlg/dot_general | solution.py:38
  110.1 1.8 %fusion.42 = f32[32,128,128]{2,1,0:T(8,128)S(1)} fusion(f32[128,128]{0,1:T(8,128)S(1)} %get-tuple-element.138, f32[32,128]{1,0:T(8,128)S(1)} %bitcast_convert_fusion.2), kind=kOutput, calls=%fused_computation.13.clone.1 | convolution fusion | flops 805863424 | bytes 2179072 | tf_op jit(solution)/shard_map/while/body/eval_jaxpr/tmg,ml->tlg/dot_general | solution.py:38
  113.5 1.8 %fusion.42 = f32[32,128,128]{2,1,0:T(8,128)S(1)} fusion(f32[128,128]{0,1:T(8,128)S(1)} %get-tuple-element.138, f32[32,128]{1,0:T(8,128)S(1)} %bitcast_convert_fusion.2), kind=kOutput, calls=%fused_computation.13.clone.1 | convolution fusion | flops 805863424 | bytes 2179072 | tf_op jit(solution)/shard_map/while/body/eval_jaxpr/tmg,ml->tlg/dot_general | solution.py:38
  121.1 2.8 %gather_fusion.4 = f32[1024,128]{1,0:T(8,128)S(1)} fusion(f32[512,128]{1,0:T(8,128)S(1)} %subtract_multiply_fusion, s32[1024]{0:T(1024)S(1)} %broadcast_clamp_fusion), kind=kCustom, calls=%fused_computation.4 | custom fusion | bytes 1052672 | tf_op jit(solution)/shard_map/gather | solution.py:107
  125.0 3.5 %all-to-all-start.2 = ((f32[64,16,128]{2,0,1:T(8,128)}), f32[64,16,128]{2,0,1:T(8,128)S(1)}, u32[]{:S(2)}, u32[]{:S(2)}) async-start(f32[64,16,128]{2,0,1:T(8,128)} %copy_select_fusion), calls=%async_computation.2 | async-start | bytes 1048576 | tf_op jit(solution)/shard_map/all_to_all | solution.py:110
  128.5 4.4 %sort.17 = (s32[1024]{0:T(1024)}, s32[1024]{0:T(1024)S(1)}) sort(s32[1024]{0:T(1024)S(1)} %bitcast.68, s32[1024]{0:T(1024)S(1)} %iota.63), dimensions={0}, to_apply=%region_7.8 | sort | flops 10240 | bytes 16384 | tf_op jit(solution)/shard_map/jit(argsort)/sort | solution.py:76
  132.9 9.3 %collective-permute-done = f32[1,64,128]{2,1,0:T(8,128)S(1)} collective-permute-done((f32[1,64,128]{2,1,0:T(8,128)S(1)}, f32[1,64,128]{2,1,0:T(8,128)S(1)}, u32[]{:S(2)}, u32[]{:S(2)}) %collective-permute-start) | collective-permute-done | bytes 32800 | tf_op jit(solution)/shard_map/ppermute | solution.py:17
  142.2 11.0 %collective-permute-start.2 = (f32[18,1,128]{2,1,0:T(1,128)S(1)}, f32[18,1,128]{2,1,0:T(1,128)S(1)}, u32[]{:S(2)}, u32[]{:S(2)}) collective-permute-start(f32[18,1,128]{2,1,0:T(1,128)S(1)} %get-tuple-element.76), channel_id=1, source_target_pairs={{1,0},{2,1},{3,2},{4,3},{5,4},{6,5},{7,6},{8,7},{9,8},{10,9},{11,1... | collective-permute-start | bytes 27656 | tf_op jit(solution)/shard_map/ppermute | solution.py:17
  153.2 1.9 %collective-permute-start.3 = (f32[18,1,128]{2,1,0:T(1,128)S(1)}, f32[18,1,128]{2,1,0:T(1,128)S(1)}, u32[]{:S(2)}, u32[]{:S(2)}) collective-permute-start(f32[18,1,128]{2,1,0:T(1,128)S(1)} %get-tuple-element.77), channel_id=1, source_target_pairs={{0,1},{1,2},{2,3},{3,4},{4,5},{5,6},{6,7},{7,8},{8,9},{9,10},{10,1... | collective-permute-start | bytes 27656 | tf_op jit(solution)/shard_map/ppermute | solution.py:16
  155.5 2.8 %gather_fusion.5 = f32[1024,128]{1,0:T(8,128)S(1)} fusion(f32[1024,128]{1,0:T(8,128)S(1)} %bitcast.57, s32[1024]{0:T(1024)S(1)} %fusion.25), kind=kCustom, calls=%fused_computation.5 | custom fusion | bytes 1052672 | tf_op jit(solution)/shard_map/gather | solution.py:113
  158.3 2.6 %collective-permute-done.3 = f32[18,1,128]{2,1,0:T(1,128)S(1)} collective-permute-done((f32[18,1,128]{2,1,0:T(1,128)S(1)}, f32[18,1,128]{2,1,0:T(1,128)S(1)}, u32[]{:S(2)}, u32[]{:S(2)}) %collective-permute-start.3) | collective-permute-done | bytes 9248 | tf_op jit(solution)/shard_map/ppermute | solution.py:16
  (128 shorter events, 40.1 us)
Async XLA Ops:
  0.6 27.3 %copy-start = (f32[16,64,128]{2,1,0:T(8,128)S(1)}, f32[16,64,128]{2,1,0:T(8,128)}, u32[]{:S(2)}) copy-start(f32[16,64,128]{2,1,0:T(8,128)} %param.10) | copy-start | bytes 1572868
  0.6 28.9 %copy-start.5 = (s32[16,64]{1,0:T(8,128)S(1)}, s32[16,64]{1,0:T(8,128)}, u32[]{:S(2)}) copy-start(s32[16,64]{1,0:T(8,128)} %param.12) | copy-start | bytes 12292
  0.7 28.9 %copy-start.3 = (f32[128,128]{1,0:T(8,128)S(1)}, f32[128,128]{1,0:T(8,128)}, u32[]{:S(2)}) copy-start(f32[128,128]{1,0:T(8,128)} %param.16) | copy-start | bytes 196612
  0.7 29.0 %copy-start.6 = (f32[128]{0:T(128)S(1)}, f32[128]{0:T(128)}, u32[]{:S(2)}) copy-start(f32[128]{0:T(128)} %param.17) | copy-start | bytes 1540
  0.7 43.7 %copy-start.2 = (f32[16,64,128]{2,1,0:T(8,128)S(1)}, f32[16,64,128]{2,1,0:T(8,128)}, u32[]{:S(2)}) copy-start(f32[16,64,128]{2,1,0:T(8,128)} %param.11) | copy-start | bytes 1572868
  10.5 24.4 %all-to-all-start = ((bf16[64,16,1]{0,2,1:T(2,128)(2,1)}), bf16[64,16,1]{0,2,1:T(2,128)(2,1)S(1)}, u32[]{:S(2)}, u32[]{:S(2)}) async-start(bf16[64,16,1]{0,2,1:T(2,128)(2,1)} %copy.10), calls=%async_computation | async-start | bytes 16384 | tf_op jit(solution)/shard_map/all_to_all | solution.py:93
  27.9 16.4 %collective-permute-start.1 = (f32[1,64,128]{2,1,0:T(8,128)S(1)}, f32[1,64,128]{2,1,0:T(8,128)S(1)}, u32[]{:S(2)}, u32[]{:S(2)}) collective-permute-start(f32[1,64,128]{2,1,0:T(8,128)S(1)} %get-tuple-element.79), channel_id=1, source_target_pairs={{0,64},{64,128},{128,192},{192,256},{256,320},{320,384},{384,448},... | collective-permute-start | bytes 98312 | tf_op jit(solution)/shard_map/ppermute | solution.py:16
  48.6 15.8 %all-to-all-start.1 = ((bf16[64,16,128]{2,0,1:T(8,128)(2,1)}), bf16[64,16,128]{2,0,1:T(8,128)(2,1)S(1)}, u32[]{:S(2)}, u32[]{:S(2)}) async-start(bf16[64,16,128]{2,0,1:T(8,128)(2,1)} %copy.14), calls=%async_computation.1 | async-start | bytes 524288 | tf_op jit(solution)/shard_map/all_to_all | solution.py:86
  123.9 4.6 %copy-start.4 = (s32[1,1,1024]{2,1,0:T(1,128)S(1)}, s32[1,1,1024]{2,1,0:T(1,128)}, u32[]{:S(2)}) copy-start(s32[1,1,1024]{2,1,0:T(1,128)} %param.14) | copy-start | bytes 12292
  125.0 30.2 %all-to-all-start.2 = ((f32[64,16,128]{2,0,1:T(8,128)}), f32[64,16,128]{2,0,1:T(8,128)S(1)}, u32[]{:S(2)}, u32[]{:S(2)}) async-start(f32[64,16,128]{2,0,1:T(8,128)} %copy_select_fusion), calls=%async_computation.2 | async-start | bytes 1048576 | tf_op jit(solution)/shard_map/all_to_all | solution.py:110
  128.5 13.8 %collective-permute-start = (f32[1,64,128]{2,1,0:T(8,128)S(1)}, f32[1,64,128]{2,1,0:T(8,128)S(1)}, u32[]{:S(2)}, u32[]{:S(2)}) collective-permute-start(f32[1,64,128]{2,1,0:T(8,128)S(1)} %get-tuple-element.78), channel_id=1, source_target_pairs={{64,0},{128,64},{192,128},{256,192},{320,256},{384,320},{448,384},... | collective-permute-start | bytes 98312 | tf_op jit(solution)/shard_map/ppermute | solution.py:17
  142.2 16.1 %collective-permute-start.2 = (f32[18,1,128]{2,1,0:T(1,128)S(1)}, f32[18,1,128]{2,1,0:T(1,128)S(1)}, u32[]{:S(2)}, u32[]{:S(2)}) collective-permute-start(f32[18,1,128]{2,1,0:T(1,128)S(1)} %get-tuple-element.76), channel_id=1, source_target_pairs={{1,0},{2,1},{3,2},{4,3},{5,4},{6,5},{7,6},{8,7},{9,8},{10,9},{11,1... | collective-permute-start | bytes 27656 | tf_op jit(solution)/shard_map/ppermute | solution.py:17
  153.2 7.7 %collective-permute-start.3 = (f32[18,1,128]{2,1,0:T(1,128)S(1)}, f32[18,1,128]{2,1,0:T(1,128)S(1)}, u32[]{:S(2)}, u32[]{:S(2)}) collective-permute-start(f32[18,1,128]{2,1,0:T(1,128)S(1)} %get-tuple-element.77), channel_id=1, source_target_pairs={{0,1},{1,2},{2,3},{3,4},{4,5},{5,6},{6,7},{7,8},{8,9},{9,10},{10,1... | collective-permute-start | bytes 27656 | tf_op jit(solution)/shard_map/ppermute | solution.py:16
  158.3 3.7 %copy-start.1 = (f32[1024,128]{1,0:T(8,128)}, f32[1024,128]{1,0:T(8,128)S(1)}, u32[]{:S(2)}) copy-start(f32[1024,128]{1,0:T(8,128)S(1)} %gather_fusion.5) | copy-start | bytes 1572868
where the time goes:
time: 162 us
  matrix products  53.1 us (33%)
  starting transfers between devices  39.4 us (24%)
  local copies, waits for them, and re-layouts  28.7 us (18%)
  waiting for transfers between devices  27.1 us (17%)
  other arithmetic  11.3 us (7%)
  between operations  1.71 us (1%)
    dot_general x16, matrix products, tile_flux(): jnp.einsum('tmg,ml->tlg', weighted, triangle, precision=lax.Precision.HIG...  28.6 us
    dot_general x16, matrix products, tile_flux(): jnp.dot(jnp.exp(-depth / cos_here[:, None, None]), insolation_by_gpoint,...  24.5 us
    all_to_all x1, starting transfers between devices, local(): lax.all_to_all(send_cos, 'gx', split_axis=1, concat_axis=1, tiled=True)  17.4 us
    ppermute x2, starting transfers between devices, extended(): after = lax.ppermute(leading, axis, down)  11 us
    all_to_all x1, waiting for transfers between devices, local(): lax.all_to_all(listed_absorb.reshape(slot_count, cycle_size, layer_tally)...  10.5 us
    ppermute x2, waiting for transfers between devices, extended(): after = lax.ppermute(leading, axis, down)  9.35 us
    gather x2, local copies, waits for them, and re-layouts, local(): listed_cos = cosine[listing]  6.88 us
    all_to_all x1, waiting for transfers between devices, local(): lax.all_to_all(send_cos, 'gx', split_axis=1, concat_axis=1, tiled=True)  4.53 us
  transfers between devices with their start and end apart: 7, of which 4 were waited for; matrix products, arithmetic and copies ran while one was open for 12% of the time, Pallas kernels for 0%

commit v1 on v0

v1 whole, which is shorter than its diff:
```python
import functools

import jax
import jax.numpy as jnp
from jax import lax
from jax.experimental import pallas as pl
from jax.experimental.pallas import tpu as pltpu
from jax.sharding import PartitionSpec as P

LOG2E = 1.4426950408889634
MESH = pl.DeviceIdType.MESH
NT = (((1,), (1,)), ((), ()))
F32, BF16, I32 = jnp.float32, jnp.bfloat16, jnp.int32
CX, CY, LEVELS = 16, 64, 128
CELLS = CX * CY
TILES = CELLS // 128
GROUP = 4
GROWS = 64
UNROLL = 32


def dot(a, b):
    return jnp.dot(a, b, preferred_element_type=F32)


def dot_nt(a, b):
    return lax.dot_general(a, b, NT, preferred_element_type=F32)


def lanes(x):
    x = x.reshape(TILES, 2, CY)
    return jnp.concatenate([x[:, 0], x[:, 1]], axis=-1)


def halves(x):
    high = x.astype(BF16)
    return high, (x - high.astype(F32)).astype(BF16)


def one_hot(rows, columns, ids):
    return lax.broadcasted_iota(I32, (rows, columns), 0) == ids


def kernel(
    kelvin, vapour, cloud, cosine, listing, count, uptake, insolation,
    after_out, heat_out,
    grid, vap, cloud_v, cos_v, list_v, count_v, up_v, ins_v,
    edge, ynear, up_t, w_t, absorb, flux, heat_v, after_v,
    in_sem, out_sem, send_sem, recv_sem,
):
    gx, gy = lax.axis_index("gx"), lax.axis_index("gy")
    nx, ny = lax.axis_size("gx"), lax.axis_size("gy")
    places = (
        (lax.rem(gx + 1, nx), gy),
        (lax.rem(gx + nx - 1, nx), gy),
        (gx, lax.rem(gy + 1, ny)),
        (gx, lax.rem(gy + ny - 1, ny)),
    )
    loads = [
        pltpu.make_async_copy(src, dst, in_sem.at[i])
        for i, (src, dst) in enumerate(
            (
                (uptake, up_v),
                (insolation, ins_v),
                (listing, list_v),
                (count, count_v),
                (cloud, cloud_v),
                (cosine, cos_v),
                (kelvin, grid.at[pl.ds(1, CX)]),
                (vapour, vap),
            )
        )
    ]
    for load in loads:
        load.start()
    barrier = pltpu.get_barrier_semaphore()
    for place in places:
        pl.semaphore_signal(barrier, inc=1, device_id=place, device_id_type=MESH)

    for load in loads[:6]:
        load.wait()
    mu = lanes(cos_v[...].astype(F32))
    speed = (-LOG2E) * (1.0 + 3.0 * lanes(cloud_v[...].astype(F32))) / mu
    ids = list_v[...]
    live = lax.broadcasted_iota(I32, (TILES, CELLS), 1) < count_v[...]
    high = (one_hot(TILES, CELLS, ids >> 7) & live).astype(F32).astype(BF16)
    low = one_hot(128, CELLS, ids & 127).astype(F32).astype(BF16)
    gain = dot_nt(high, low) * mu
    up_t[...] = up_v[...].T
    w_t[...] = jnp.broadcast_to(jnp.log2(ins_v[...]), (128, 128)).T

    for load in loads[6:]:
        load.wait()
    for x in range(CX):
        edge[0, pl.ds(x, 1), :] = grid[x + 1, pl.ds(CY - 1, 1), :]
        edge[1, pl.ds(x, 1), :] = grid[x + 1, pl.ds(0, 1), :]
    pl.semaphore_wait(barrier, 4)
    sources = (grid.at[CX], grid.at[1], edge.at[0], edge.at[1])
    targets = (grid.at[0], grid.at[CX + 1], ynear.at[0], ynear.at[1])
    sends = [
        pltpu.make_async_remote_copy(
            src_ref=sources[i],
            dst_ref=targets[i],
            send_sem=send_sem.at[i],
            recv_sem=recv_sem.at[i],
            device_id=places[i],
            device_id_type=MESH,
        )
        for i in range(4)
    ]
    for send in sends:
        send.start()

    eye = one_hot(128, 128, lax.broadcasted_iota(I32, (128, 128), 1)).astype(F32).astype(BF16)
    for t in range(TILES):
        warm = grid[2 * t + 1 : 2 * t + 3].reshape(128, LEVELS)
        amount = vap[2 * t : 2 * t + 2].reshape(128, LEVELS)
        plain = (amount * jnp.exp(0.25 * warm)).astype(BF16)
        absorb[t] = dot_nt(eye, plain) * speed[t : t + 1]

    def some_gpoints(q, p, first):
        at = pl.ds(pl.multiple_of(p * GROWS, GROWS), GROWS)
        start = w_t[at, :]

        def fold(e):
            return jnp.sum(e.reshape(GROWS // 8, 8, 128), axis=0)

        above = fold(jnp.exp2(start))
        for t in range(GROUP):
            flux[t, :8] = above if first else flux[t, :8] + above

        def levels(b, carry):
            ks, depth = carry
            depth = list(depth)
            for u in range(UNROLL):
                level = b * UNROLL + u
                kb = jnp.broadcast_to(ks[:, u : u + 1], (GROWS, 128))
                for t in range(GROUP):
                    row = absorb[q * GROUP + t, pl.ds(level, 1), :]
                    depth[t] = depth[t] + kb * row
                    total = fold(jnp.exp2(depth[t]))
                    to = (t, pl.ds(pl.multiple_of(level * 8 + 8, 8), 8), slice(None))
                    flux[to] = total if first else flux[to] + total
            return pltpu.roll(ks, 128 - UNROLL, 1), tuple(depth)

        lax.fori_loop(0, LEVELS // UNROLL, levels, (up_t[at, :], (start,) * GROUP))

    sums = one_hot(32, 256, lax.broadcasted_iota(I32, (32, 256), 1) >> 3).astype(F32).astype(BF16)
    yrow = lax.broadcasted_iota(I32, (CY, 128), 0)
    outs = []
    for q in range(TILES // GROUP):
        some_gpoints(q, 0, True)
        for p in range(1, 128 // GROWS):
            some_gpoints(q, p, False)
        if q == 0:
            for send in sends:
                send.wait()
        for t in range(GROUP):
            tile = q * GROUP + t
            parts = []
            for r in range(4):
                drop = flux[t, r * 256 : r * 256 + 256] - flux[t, r * 256 + 8 : r * 256 + 264]
                h, l = halves(drop)
                parts.append(dot(sums, h) + dot(sums, l))
            gained = (jnp.concatenate(parts, axis=0) * gain[tile : tile + 1]).T
            for i in range(2):
                x = 2 * tile + i
                here = grid[x + 1]
                south = jnp.where(yrow == 0, ynear[0, x : x + 1, :], pltpu.roll(here, 1, 0))
                north = jnp.where(yrow == CY - 1, ynear[1, x : x + 1, :], pltpu.roll(here, CY - 1, 0))
                near = grid[x + 2] + grid[x] + north + south
                heat = gained[i * CY : i * CY + CY]
                heat_v[x] = heat
                after_v[x] = here + 0.2 * (near - 4.0 * here) + heat
        for i, (src, dst) in enumerate(((after_v, after_out), (heat_v, heat_out))):
            span = pl.ds(q * 2 * GROUP, 2 * GROUP)
            out = pltpu.make_async_copy(src.at[span], dst.at[span], out_sem.at[2 * q + i])
            out.start()
            outs.append(out)
    for out in outs:
        out.wait()


def local(kelvin, vapour, cloud, cosine, listing, count, uptake, insolation):
    hbm = pl.BlockSpec(memory_space=pltpu.HBM)
    vmem = pltpu.VMEM
    block = jax.ShapeDtypeStruct((CX, CY, LEVELS), F32)
    return pl.pallas_call(
        kernel,
        out_shape=(block, block),
        in_specs=[hbm] * 8,
        out_specs=(hbm, hbm),
        scratch_shapes=[
            vmem((CX + 2, CY, LEVELS), F32),
            vmem((CX, CY, LEVELS), F32),
            vmem((CX, CY), I32),
            vmem((CX, CY), BF16),
            vmem((1, CELLS), I32),
            vmem((1, 1), I32),
            vmem((128, 128), F32),
            vmem((1, 128), F32),
            vmem((2, CX, LEVELS), F32),
            vmem((2, CX, LEVELS), F32),
            vmem((128, 128), F32),
            vmem((128, 128), F32),
            vmem((TILES, LEVELS, 128), F32),
            vmem((GROUP, 8 * LEVELS + 8, 128), F32),
            vmem((CX, CY, LEVELS), F32),
            vmem((CX, CY, LEVELS), F32),
            pltpu.SemaphoreType.DMA((8,)),
            pltpu.SemaphoreType.DMA((2 * TILES // GROUP,)),
            pltpu.SemaphoreType.DMA((4,)),
            pltpu.SemaphoreType.DMA((4,)),
        ],
        compiler_params=pltpu.CompilerParams(
            collective_id=0, has_side_effects=True, vmem_limit_bytes=60 * 2**20
        ),
        cost_estimate=pl.CostEstimate(
            flops=4 * CELLS * 128 * 128, bytes_accessed=2**21, transcendentals=CELLS * 128 * 128
        ),
    )(
        kelvin,
        vapour,
        cloud,
        cosine,
        listing.reshape(1, CELLS),
        count,
        uptake,
        insolation.reshape(1, 128),
    )


def solution(mesh):
    in_specs = (
        P("gx", "gy", None),
        P("gx", "gy", None),
        P("gx", "gy"),
        P("gx", "gy"),
        P("gx", "gy", None),
        P("gx", "gy"),
        P(),
        P(),
    )
    out_specs = (P("gx", "gy", None), P("gx", "gy", None))
    return jax.shard_map(local, mesh=mesh, in_specs=in_specs, out_specs=out_specs, check_vma=False)
```

time: 162 us -> 35.7 us (0.22)
  matrix products: 53.1 us -> 0 us
  starting transfers between devices: 39.4 us -> 0 us
  Pallas kernels: 0 us -> 31.5 us
  waiting for transfers between devices: 27.1 us -> 0 us
  local copies, waits for them, and re-layouts: 28.7 us -> 2.74 us
  other arithmetic: 11.3 us -> 0 us
    dot_general x32 -> x0, matrix products: 53.1 us -> none  [the longest x16 28.6 us: tile_flux(): jnp.einsum('tmg,ml->tlg', weighted, triangle, precision=lax.Precision.HIG...]
    pallas_call x0 -> x1, Pallas kernels: none -> 31.5 us  [local(): pl.pallas_call(kernel, out_shape=(block, block), in_specs=[hbm] * 8, out_...]
    all_to_all x3 -> x0, starting transfers between devices: 24.9 us -> none  [the longest x1 17.4 us: local(): lax.all_to_all(send_cos, 'gx', split_axis=1, concat_axis=1, tiled=True)]
    gather x7 -> x0, local copies, waits for them, and re-layouts: 20.6 us -> none  [the longest x2 6.88 us: local(): listed_cos = cosine[listing]]
    all_to_all x3 -> x0, waiting for transfers between devices: 15.1 us -> none  [the longest x1 10.5 us: local(): lax.all_to_all(listed_absorb.reshape(slot_count, cycle_size, layer_tally)...]
    ppermute x4 -> x0, starting transfers between devices: 14.6 us -> none  [the longest x2 11 us: extended(): after = lax.ppermute(leading, axis, down)]
    ppermute x4 -> x0, waiting for transfers between devices: 12 us -> none  [the longest x2 9.35 us: extended(): after = lax.ppermute(leading, axis, down)]
    sort x1 -> x0, other arithmetic: 4.37 us -> none  [local(): ranks = jnp.argsort(listing)]
  transfers between devices with their start and end apart: 7 -> 0, of which waited for: 4 -> 0; matrix products, arithmetic and copies ran while one was open for 12% -> 0% of each run, Pallas kernels for 0% -> 0%
where the time goes in v1:
time: 35.7 us; the launch traced here: 35.5 us
  Pallas kernels  31.5 us (88%)
  local copies, waits for them, and re-layouts  2.74 us (8%)
  between operations  1.29 us (4%)
    pallas_call x1, Pallas kernels, local(): pl.pallas_call(kernel, out_shape=(block, block), in_specs=[hbm] * 8, out_...  31.5 us
    unnamed x4, local copies, waits for them, and re-layouts  2.74 us

profile of v1, /device:TPU:1, one launch (start us, length us, event | category | flops | bytes accessed | tf_op | source)
XLA Modules:
  0.0 35.5 jit_solution(14575665366235917265)
XLA Ops:
  1.3 31.5 %shard_map.95 = (f32[16,64,128]{2,1,0:T(8,128)}, f32[16,64,128]{2,1,0:T(8,128)}) custom-call(f32[16,64,128]{2,1,0:T(8,128)} %kelvin.1, f32[16,64,128]{2,1,0:T(8,128)} %vapour.1, s32[16,64]{1,0:T(8,128)} %cloud.1, bf16[16,64]{1,0:T(8,128)(2,1)} %cosine.1, s32[1,1024]{1,0:T(1,128)} %bitcast.2, s32[1,1]{1,0:T(1,128)S(6)} %copy.12.count, f32[128,128]{1,0:T(8,128)} %uptake.1, ...), custom_call_target="tpu_custom_call" | custom-call | flops 67108864 | bytes 2097152 | tf_op jit(solution)/shard_map/pallas_call | solution.py:188
  32.7 0.0 copy-start
  32.8 1.9 %copy.13 = f32[16,64,128]{2,1,0:T(8,128)} copy(f32[16,64,128]{2,1,0:T(8,128)} %get-tuple-element.4) | data formatting | bytes 1048576
  34.7 0.0 copy-done
  34.7 0.8 %copy.14 = f32[16,64,128]{2,1,0:T(8,128)} copy(f32[16,64,128]{2,1,0:T(8,128)S(1)} %copy-done) | data formatting | bytes 1048576
Async XLA Ops:
  32.7 2.0 %copy-start = (f32[16,64,128]{2,1,0:T(8,128)S(1)}, f32[16,64,128]{2,1,0:T(8,128)}, u32[]{:S(2)}) copy-start(f32[16,64,128]{2,1,0:T(8,128)} %get-tuple-element.5) | copy-start | bytes 1572868

commit v2 on v1

--- a/solution.py
+++ b/solution.py
@@ -16,6 +16,7 @@
 TILES = CELLS // 128
 GROUP = 4
 GROWS = 64
+PLANES = 8
 UNROLL = 32
 
 
@@ -43,19 +44,62 @@
 
 def kernel(
     kelvin, vapour, cloud, cosine, listing, count, uptake, insolation,
-    after_out, heat_out,
+    still_out, high_out, low_out,
     grid, vap, cloud_v, cos_v, list_v, count_v, up_v, ins_v,
-    edge, ynear, up_t, w_t, absorb, flux, heat_v, after_v,
+    ynear, up_t, w_t, absorb, flux, high_v, low_v, still_v,
     in_sem, out_sem, send_sem, recv_sem,
 ):
     gx, gy = lax.axis_index("gx"), lax.axis_index("gy")
     nx, ny = lax.axis_size("gx"), lax.axis_size("gy")
-    places = (
-        (lax.rem(gx + 1, nx), gy),
-        (lax.rem(gx + nx - 1, nx), gy),
-        (gx, lax.rem(gy + 1, ny)),
-        (gx, lax.rem(gy + ny - 1, ny)),
+    z = lax.rem(gy, PLANES)
+    even, first = lax.rem(gx, 2) == 0, gy == 0
+    late = (
+        (z == 0) | (z == PLANES - 1),
+        z >= 2,
+        even & ((gx > 0) | first),
+        even | ((gx == nx - 1) & (gy > 0)),
     )
+    early = tuple(jnp.logical_not(x) for x in late)
+    west, east = (lax.rem(gx + nx - 1, nx), gy), (lax.rem(gx + 1, nx), gy)
+    south, north = (gx, lax.rem(gy + ny - 1, ny)), (gx, lax.rem(gy + 1, ny))
+    neighbours = (north, south, west, east)
+    mine = (kelvin.at[:, CY - 1], kelvin.at[:, 0], kelvin.at[0], kelvin.at[CX - 1])
+    lands = (ynear.at[0], ynear.at[1], grid.at[CX + 1], grid.at[0])
+    back = (1, 0, 3, 2)
+    sends = [
+        pltpu.make_async_remote_copy(
+            src_ref=mine[i],
+            dst_ref=lands[i],
+            send_sem=send_sem.at[i],
+            recv_sem=recv_sem.at[i],
+            device_id=neighbours[i],
+            device_id_type=MESH,
+        )
+        for i in range(4)
+    ]
+    barrier = pltpu.get_barrier_semaphore()
+
+    def greet(i):
+        pl.semaphore_signal(barrier, inc=1, device_id=neighbours[i], device_id_type=MESH)
+
+    def send(i):
+        sends[i].start()
+
+    def answer(i):
+        sends[back[i]].wait_recv()
+        sends[i].start()
+
+    def receive(i):
+        sends[back[i]].wait_recv()
+
+    def each(when, act, order=range(4)):
+        for i in order:
+            pl.when(when[i])(functools.partial(act, i))
+
+    greeted = sum(x.astype(I32) for x in late)
+    each(early, greet)
+    pl.when(greeted > 0)(lambda: pl.semaphore_wait(barrier, greeted))
+    each(late, send)
     loads = [
         pltpu.make_async_copy(src, dst, in_sem.at[i])
         for i, (src, dst) in enumerate(
@@ -73,10 +117,6 @@
     ]
     for load in loads:
         load.start()
-    barrier = pltpu.get_barrier_semaphore()
-    for place in places:
-        pl.semaphore_signal(barrier, inc=1, device_id=place, device_id_type=MESH)
-
     for load in loads[:6]:
         load.wait()
     mu = lanes(cos_v[...].astype(F32))
@@ -91,26 +131,6 @@
 
     for load in loads[6:]:
         load.wait()
-    for x in range(CX):
-        edge[0, pl.ds(x, 1), :] = grid[x + 1, pl.ds(CY - 1, 1), :]
-        edge[1, pl.ds(x, 1), :] = grid[x + 1, pl.ds(0, 1), :]
-    pl.semaphore_wait(barrier, 4)
-    sources = (grid.at[CX], grid.at[1], edge.at[0], edge.at[1])
-    targets = (grid.at[0], grid.at[CX + 1], ynear.at[0], ynear.at[1])
-    sends = [
-        pltpu.make_async_remote_copy(
-            src_ref=sources[i],
-            dst_ref=targets[i],
-            send_sem=send_sem.at[i],
-            recv_sem=recv_sem.at[i],
-            device_id=places[i],
-            device_id_type=MESH,
-        )
-        for i in range(4)
-    ]
-    for send in sends:
-        send.start()
-
     eye = one_hot(128, 128, lax.broadcasted_iota(I32, (128, 128), 1)).astype(F32).astype(BF16)
     for t in range(TILES):
         warm = grid[2 * t + 1 : 2 * t + 3].reshape(128, LEVELS)
@@ -153,8 +173,7 @@
         for p in range(1, 128 // GROWS):
             some_gpoints(q, p, False)
         if q == 0:
-            for send in sends:
-                send.wait()
+            pl.when(z >= 2)(functools.partial(each, early, answer, (2, 3, 0, 1)))
         for t in range(GROUP):
             tile = q * GROUP + t
             parts = []
@@ -166,17 +185,31 @@
             for i in range(2):
                 x = 2 * tile + i
                 here = grid[x + 1]
-                south = jnp.where(yrow == 0, ynear[0, x : x + 1, :], pltpu.roll(here, 1, 0))
-                north = jnp.where(yrow == CY - 1, ynear[1, x : x + 1, :], pltpu.roll(here, CY - 1, 0))
-                near = grid[x + 2] + grid[x] + north + south
-                heat = gained[i * CY : i * CY + CY]
-                heat_v[x] = heat
-                after_v[x] = here + 0.2 * (near - 4.0 * here) + heat
-        for i, (src, dst) in enumerate(((after_v, after_out), (heat_v, heat_out))):
-            span = pl.ds(q * 2 * GROUP, 2 * GROUP)
+                near = jnp.where(yrow == 0, 0.0, pltpu.roll(here, 1, 0))
+                near += jnp.where(yrow == CY - 1, 0.0, pltpu.roll(here, CY - 1, 0))
+                if x > 0:
+                    near += grid[x]
+                if x < CX - 1:
+                    near += grid[x + 2]
+                high_v[x], low_v[x] = halves(gained[i * CY : i * CY + CY])
+                still_v[x] = here + 0.2 * (near - 4.0 * here)
+        span = pl.ds(q * 2 * GROUP, 2 * GROUP)
+        for i, (src, dst) in enumerate(((high_v, high_out), (low_v, low_out))):
             out = pltpu.make_async_copy(src.at[span], dst.at[span], out_sem.at[2 * q + i])
             out.start()
             outs.append(out)
+    pl.when(z < 2)(functools.partial(each, early, answer, (2, 3, 0, 1)))
+    each(late, receive)
+    still_v[0] += 0.2 * grid[0]
+    still_v[CX - 1] += 0.2 * grid[CX + 1]
+    for x in range(CX):
+        still_v[x, :1] += 0.2 * ynear[0, x : x + 1]
+        still_v[x, CY - 1 :] += 0.2 * ynear[1, x : x + 1]
+    out = pltpu.make_async_copy(still_v, still_out, out_sem.at[2 * TILES // GROUP])
+    out.start()
+    for i in range(4):
+        sends[i].wait_send()
+    out.wait()
     for out in outs:
         out.wait()
 
@@ -184,12 +217,12 @@
 def local(kelvin, vapour, cloud, cosine, listing, count, uptake, insolation):
     hbm = pl.BlockSpec(memory_space=pltpu.HBM)
     vmem = pltpu.VMEM
-    block = jax.ShapeDtypeStruct((CX, CY, LEVELS), F32)
-    return pl.pallas_call(
+    block = (CX, CY, LEVELS)
+    still, high, low = pl.pallas_call(
         kernel,
-        out_shape=(block, block),
+        out_shape=tuple(jax.ShapeDtypeStruct(block, x) for x in (F32, BF16, BF16)),
         in_specs=[hbm] * 8,
-        out_specs=(hbm, hbm),
+        out_specs=(hbm, hbm, hbm),
         scratch_shapes=[
             vmem((CX + 2, CY, LEVELS), F32),
             vmem((CX, CY, LEVELS), F32),
@@ -200,15 +233,15 @@
             vmem((128, 128), F32),
             vmem((1, 128), F32),
             vmem((2, CX, LEVELS), F32),
-            vmem((2, CX, LEVELS), F32),
             vmem((128, 128), F32),
             vmem((128, 128), F32),
             vmem((TILES, LEVELS, 128), F32),
             vmem((GROUP, 8 * LEVELS + 8, 128), F32),
-            vmem((CX, CY, LEVELS), F32),
-            vmem((CX, CY, LEVELS), F32),
+            vmem(block, BF16),
+            vmem(block, BF16),
+            vmem(block, F32),
             pltpu.SemaphoreType.DMA((8,)),
-            pltpu.SemaphoreType.DMA((2 * TILES // GROUP,)),
+            pltpu.SemaphoreType.DMA((2 * TILES // GROUP + 1,)),
             pltpu.SemaphoreType.DMA((4,)),
             pltpu.SemaphoreType.DMA((4,)),
         ],
@@ -228,6 +261,8 @@
         uptake,
         insolation.reshape(1, 128),
     )
+    heat = high.astype(F32) + low.astype(F32)
+    return still + heat, heat
 
 
 def solution(mesh):

time: 35.7 us -> 26.5 us (0.74)
  the two profiles are of different devices: /device:TPU:1 before, /device:TPU:112 now
where the time goes in v2:
time: 26.5 us; the launch traced here: 26.3 us
  Pallas kernels  22.8 us (86%)
  other arithmetic  2.28 us (9%)
  between operations  1.29 us (5%)
    pallas_call x1, Pallas kernels, local(): pl.pallas_call(kernel, out_shape=tuple((jax.ShapeDtypeStruct(block, x) fo...  22.8 us
    add x1, other arithmetic, local(): return (still + heat, heat)  2.28 us

profile of v2, /device:TPU:112, one launch (start us, length us, event | category | flops | bytes accessed | tf_op | source)
XLA Modules:
  0.0 26.3 jit_solution(4595342853409802136)
XLA Ops:
  1.3 22.8 %shard_map.95 = (f32[16,64,128]{2,1,0:T(8,128)}, bf16[16,64,128]{2,1,0:T(8,128)(2,1)}, bf16[16,64,128]{2,1,0:T(8,128)(2,1)}) custom-call(f32[16,64,128]{2,1,0:T(8,128)} %kelvin.1, f32[16,64,128]{2,1,0:T(8,128)} %vapour.1, s32[16,64]{1,0:T(8,128)} %cloud.1, bf16[16,64]{1,0:T(8,128)(2,1)} %cosine.1, s32[1,1024]{1,0:T(1,128)} %bitcast.2, ...), custom_call_target="tpu_custom_call" | custom-call | flops 67108864 | bytes 2097152 | tf_op jit(solution)/shard_map/pallas_call | solution.py:221
  24.1 2.3 %fusion = (f32[16,64,128]{2,1,0:T(8,128)}, f32[16,64,128]{2,1,0:T(8,128)}) fusion(f32[16,64,128]{2,1,0:T(8,128)} %get-tuple-element.5, bf16[16,64,128]{2,1,0:T(8,128)(2,1)} %get-tuple-element.7, bf16[16,64,128]{2,1,0:T(8,128)(2,1)} %get-tuple-element.6), kind=kLoop, calls=%fused_computation.1 | loop fusion | flops 524288 | bytes 2097152 | tf_op jit(solution)/shard_map/add | solution.py:265

commit v3 on v2

--- a/solution.py
+++ b/solution.py
@@ -17,6 +17,7 @@
 GROUP = 4
 GROWS = 64
 PLANES = 8
+PIECES = 4
 UNROLL = 32
 
 
@@ -44,10 +45,10 @@
 
 def kernel(
     kelvin, vapour, cloud, cosine, listing, count, uptake, insolation,
-    still_out, high_out, low_out,
+    after_out, heat_out, south_out, north_out,
     grid, vap, cloud_v, cos_v, list_v, count_v, up_v, ins_v,
-    ynear, up_t, w_t, absorb, flux, high_v, low_v, still_v,
-    in_sem, out_sem, send_sem, recv_sem,
+    up_t, w_t, absorb, flux, heat_v, after_v,
+    in_sem, out_sem, send_sem, recv_sem, here_sem,
 ):
     gx, gy = lax.axis_index("gx"), lax.axis_index("gy")
     nx, ny = lax.axis_size("gx"), lax.axis_size("gy")
@@ -64,7 +65,7 @@
     south, north = (gx, lax.rem(gy + ny - 1, ny)), (gx, lax.rem(gy + 1, ny))
     neighbours = (north, south, west, east)
     mine = (kelvin.at[:, CY - 1], kelvin.at[:, 0], kelvin.at[0], kelvin.at[CX - 1])
-    lands = (ynear.at[0], ynear.at[1], grid.at[CX + 1], grid.at[0])
+    lands = (south_out, north_out, grid.at[CX + 1], grid.at[0])
     back = (1, 0, 3, 2)
     sends = [
         pltpu.make_async_remote_copy(
@@ -82,11 +83,16 @@
     def greet(i):
         pl.semaphore_signal(barrier, inc=1, device_id=neighbours[i], device_id_type=MESH)
 
+    def call(i):
+        pl.semaphore_signal(
+            here_sem.at[back[i]], inc=1, device_id=neighbours[i], device_id_type=MESH
+        )
+
     def send(i):
         sends[i].start()
 
     def answer(i):
-        sends[back[i]].wait_recv()
+        pl.semaphore_wait(here_sem.at[i], 1)
         sends[i].start()
 
     def receive(i):
@@ -99,6 +105,7 @@
     greeted = sum(x.astype(I32) for x in late)
     each(early, greet)
     pl.when(greeted > 0)(lambda: pl.semaphore_wait(barrier, greeted))
+    each(late, call)
     each(late, send)
     loads = [
         pltpu.make_async_copy(src, dst, in_sem.at[i])
@@ -173,7 +180,8 @@
         for p in range(1, 128 // GROWS):
             some_gpoints(q, p, False)
         if q == 0:
-            pl.when(z >= 2)(functools.partial(each, early, answer, (2, 3, 0, 1)))
+            pl.when(gy > 0)(functools.partial(each, early, answer, (2, 3)))
+            pl.when(z >= 2)(functools.partial(each, early, answer, (0, 1)))
         for t in range(GROUP):
             tile = q * GROUP + t
             parts = []
@@ -191,38 +199,66 @@
                     near += grid[x]
                 if x < CX - 1:
                     near += grid[x + 2]
-                high_v[x], low_v[x] = halves(gained[i * CY : i * CY + CY])
-                still_v[x] = here + 0.2 * (near - 4.0 * here)
+                heat = gained[i * CY : i * CY + CY]
+                heat_v[x] = heat
+                after_v[x] = here + 0.2 * (near - 4.0 * here) + heat
         span = pl.ds(q * 2 * GROUP, 2 * GROUP)
-        for i, (src, dst) in enumerate(((high_v, high_out), (low_v, low_out))):
-            out = pltpu.make_async_copy(src.at[span], dst.at[span], out_sem.at[2 * q + i])
-            out.start()
-            outs.append(out)
-    pl.when(z < 2)(functools.partial(each, early, answer, (2, 3, 0, 1)))
-    each(late, receive)
-    still_v[0] += 0.2 * grid[0]
-    still_v[CX - 1] += 0.2 * grid[CX + 1]
-    for x in range(CX):
-        still_v[x, :1] += 0.2 * ynear[0, x : x + 1]
-        still_v[x, CY - 1 :] += 0.2 * ynear[1, x : x + 1]
-    out = pltpu.make_async_copy(still_v, still_out, out_sem.at[2 * TILES // GROUP])
+        out = pltpu.make_async_copy(heat_v.at[span], heat_out.at[span], out_sem.at[q])
+        out.start()
+        outs.append(out)
+    pl.when(gy == 0)(functools.partial(each, early, answer, (2, 3)))
+    receive(2)
+    receive(3)
+    after_v[0] += 0.2 * grid[0]
+    after_v[CX - 1] += 0.2 * grid[CX + 1]
+    out = pltpu.make_async_copy(after_v, after_out, out_sem.at[TILES // GROUP])
     out.start()
+    outs.append(out)
+    pl.when(z < 2)(functools.partial(each, early, answer, (0, 1)))
+    receive(0)
+    receive(1)
     for i in range(4):
         sends[i].wait_send()
-    out.wait()
     for out in outs:
         out.wait()
+
+
+def finish(after, heat, south, north, after_out, heat_out, after_v, heat_v, edges, in_sem, out_sem):
+    copy = pltpu.make_async_copy
+    loads = [copy(south, edges.at[0], in_sem.at[0]), copy(north, edges.at[1], in_sem.at[1])]
+    stores = []
+    step = CX // PIECES
+    for i in range(PIECES):
+        span = pl.ds(i * step, step)
+        loads.append(copy(after.at[span], after_v.at[span], in_sem.at[2 * i + 2]))
+        loads.append(copy(heat.at[span], heat_v.at[span], in_sem.at[2 * i + 3]))
+        stores.append(copy(after_v.at[span], after_out.at[span], out_sem.at[2 * i]))
+        stores.append(copy(heat_v.at[span], heat_out.at[span], out_sem.at[2 * i + 1]))
+    for load in loads:
+        load.start()
+    loads[0].wait()
+    loads[1].wait()
+    for i in range(PIECES):
+        loads[2 * i + 2].wait()
+        for x in range(i * step, i * step + step):
+            after_v[x, :1] += 0.2 * edges[0, x : x + 1]
+            after_v[x, CY - 1 :] += 0.2 * edges[1, x : x + 1]
+        stores[2 * i].start()
+        loads[2 * i + 3].wait()
+        stores[2 * i + 1].start()
+    for store in stores:
+        store.wait()
 
 
 def local(kelvin, vapour, cloud, cosine, listing, count, uptake, insolation):
     hbm = pl.BlockSpec(memory_space=pltpu.HBM)
     vmem = pltpu.VMEM
-    block = (CX, CY, LEVELS)
-    still, high, low = pl.pallas_call(
+    block, edge = (CX, CY, LEVELS), (CX, LEVELS)
+    after, heat, south, north = pl.pallas_call(
         kernel,
-        out_shape=tuple(jax.ShapeDtypeStruct(block, x) for x in (F32, BF16, BF16)),
+        out_shape=tuple(jax.ShapeDtypeStruct(x, F32) for x in (block, block, edge, edge)),
         in_specs=[hbm] * 8,
-        out_specs=(hbm, hbm, hbm),
+        out_specs=(hbm,) * 4,
         scratch_shapes=[
             vmem((CX + 2, CY, LEVELS), F32),
             vmem((CX, CY, LEVELS), F32),
@@ -232,18 +268,17 @@
             vmem((1, 1), I32),
             vmem((128, 128), F32),
             vmem((1, 128), F32),
-            vmem((2, CX, LEVELS), F32),
             vmem((128, 128), F32),
             vmem((128, 128), F32),
             vmem((TILES, LEVELS, 128), F32),
             vmem((GROUP, 8 * LEVELS + 8, 128), F32),
-            vmem(block, BF16),
-            vmem(block, BF16),
+            vmem(block, F32),
             vmem(block, F32),
             pltpu.SemaphoreType.DMA((8,)),
-            pltpu.SemaphoreType.DMA((2 * TILES // GROUP + 1,)),
+            pltpu.SemaphoreType.DMA((TILES // GROUP + 1,)),
             pltpu.SemaphoreType.DMA((4,)),
             pltpu.SemaphoreType.DMA((4,)),
+            pltpu.SemaphoreType.REGULAR((4,)),
         ],
         compiler_params=pltpu.CompilerParams(
             collective_id=0, has_side_effects=True, vmem_limit_bytes=60 * 2**20
@@ -261,8 +296,20 @@
         uptake,
         insolation.reshape(1, 128),
     )
-    heat = high.astype(F32) + low.astype(F32)
-    return still + heat, heat
+    return pl.pallas_call(
+        finish,
+        out_shape=tuple(jax.ShapeDtypeStruct(block, F32) for _ in range(2)),
+        in_specs=[hbm] * 4,
+        out_specs=(hbm,) * 2,
+        scratch_shapes=[
+            vmem(block, F32),
+            vmem(block, F32),
+            vmem((2, CX, LEVELS), F32),
+            pltpu.SemaphoreType.DMA((2 * PIECES + 2,)),
+            pltpu.SemaphoreType.DMA((2 * PIECES,)),
+        ],
+        compiler_params=pltpu.CompilerParams(vmem_limit_bytes=60 * 2**20),
+    )(after, heat, south, north)
 
 
 def solution(mesh):

time: 26.5 us -> 24.9 us (0.940)
  other arithmetic: 2.28 us -> 0 us
  Pallas kernels: 22.8 us -> 23.5 us
    add x1 -> x0, other arithmetic: 2.28 us -> none  [local(): return (still + heat, heat)]
    pallas_call x1 -> x2, Pallas kernels: 22.8 us -> 23.5 us  [the longest x1 21.3 us: local(): pl.pallas_call(kernel, out_shape=tuple((jax.ShapeDtypeStruct(x, F32) for...]
where the time goes in v3:
time: 24.9 us; the launch traced here: 24.7 us
  Pallas kernels  23.5 us (94%)
  between operations  1.29 us (5%)
    pallas_call x1, Pallas kernels, local(): pl.pallas_call(kernel, out_shape=tuple((jax.ShapeDtypeStruct(x, F32) for...  21.3 us
    pallas_call x1, Pallas kernels, local(): pl.pallas_call(finish, out_shape=tuple((jax.ShapeDtypeStruct(block, F32)...  2.14 us

profile of v3, /device:TPU:112, one launch (start us, length us, event | category | flops | bytes accessed | tf_op | source)
XLA Modules:
  0.0 24.7 jit_solution(12439582512423235584)
XLA Ops:
  1.3 21.3 %shard_map.95 = (f32[16,64,128]{2,1,0:T(8,128)}, f32[16,64,128]{2,1,0:T(8,128)}, f32[16,128]{1,0:T(8,128)}, f32[16,128]{1,0:T(8,128)}) custom-call(f32[16,64,128]{2,1,0:T(8,128)} %kelvin.1, f32[16,64,128]{2,1,0:T(8,128)} %vapour.1, s32[16,64]{1,0:T(8,128)} %cloud.1, bf16[16,64]{1,0:T(8,128)(2,1)} %cosine.1, s32[1,1024]{1,0:T(1,128)} %bitcast.2, ...), custom_call_target="tpu_custom_call" | custom-call | flops 67108864 | bytes 2097152 | tf_op jit(solution)/shard_map/pallas_call | solution.py:257
  22.6 2.1 %shard_map.96 = (f32[16,64,128]{2,1,0:T(8,128)}, f32[16,64,128]{2,1,0:T(8,128)}) custom-call(f32[16,64,128]{2,1,0:T(8,128)} %get-tuple-element.6.after, f32[16,64,128]{2,1,0:T(8,128)} %get-tuple-element.7.heat, f32[16,128]{1,0:T(8,128)} %get-tuple-element.8.south, f32[16,128]{1,0:T(8,128)} %get-tuple-element.9.north), custom_call_target="tpu_custom_call" | custom-call | tf_op jit(solution)/shard_map/pallas_call | solution.py:299

commit v4 on v3

--- a/solution.py
+++ b/solution.py
@@ -17,7 +17,7 @@
 GROUP = 4
 GROWS = 64
 PLANES = 8
-PIECES = 4
+PIECES = 2
 UNROLL = 32
 
 
@@ -57,8 +57,8 @@
     late = (
         (z == 0) | (z == PLANES - 1),
         z >= 2,
-        even & ((gx > 0) | first),
-        even | ((gx == nx - 1) & (gy > 0)),
+        even & (((gx > 0) & (gx <= nx // 2)) | ((gx == 0) & first)),
+        even | ((gx > nx // 2) & ((gx < nx - 1) | (gy > 0))),
     )
     early = tuple(jnp.logical_not(x) for x in late)
     west, east = (lax.rem(gx + nx - 1, nx), gy), (lax.rem(gx + 1, nx), gy)

time: 24.9 us -> 24.8 us (level)
  the two profiles are of different devices: /device:TPU:112 before, /device:TPU:97 now
where the time goes in v4:
time: 24.8 us; the launch traced here: 24.6 us
  Pallas kernels  23.3 us (94%)
  between operations  1.29 us (5%)
    pallas_call x1, Pallas kernels, local(): pl.pallas_call(kernel, out_shape=tuple((jax.ShapeDtypeStruct(x, F32) for...  21.3 us
    pallas_call x1, Pallas kernels, local(): pl.pallas_call(finish, out_shape=tuple((jax.ShapeDtypeStruct(block, F32)...  2.04 us

profile of v4, /device:TPU:97, one launch (start us, length us, event | category | flops | bytes accessed | tf_op | source)
XLA Modules:
  0.0 24.6 jit_solution(9814658869611754381)
XLA Ops:
  1.3 21.3 %shard_map.95 = (f32[16,64,128]{2,1,0:T(8,128)}, f32[16,64,128]{2,1,0:T(8,128)}, f32[16,128]{1,0:T(8,128)}, f32[16,128]{1,0:T(8,128)}) custom-call(f32[16,64,128]{2,1,0:T(8,128)} %kelvin.1, f32[16,64,128]{2,1,0:T(8,128)} %vapour.1, s32[16,64]{1,0:T(8,128)} %cloud.1, bf16[16,64]{1,0:T(8,128)(2,1)} %cosine.1, s32[1,1024]{1,0:T(1,128)} %bitcast.2, ...), custom_call_target="tpu_custom_call" | custom-call | flops 67108864 | bytes 2097152 | tf_op jit(solution)/shard_map/pallas_call | solution.py:257
  22.6 2.0 %shard_map.96 = (f32[16,64,128]{2,1,0:T(8,128)}, f32[16,64,128]{2,1,0:T(8,128)}) custom-call(f32[16,64,128]{2,1,0:T(8,128)} %get-tuple-element.6.after, f32[16,64,128]{2,1,0:T(8,128)} %get-tuple-element.7.heat, f32[16,128]{1,0:T(8,128)} %get-tuple-element.8.south, f32[16,128]{1,0:T(8,128)} %get-tuple-element.9.north), custom_call_target="tpu_custom_call" | custom-call | tf_op jit(solution)/shard_map/pallas_call | solution.py:299

commit v5 on v4

--- a/solution.py
+++ b/solution.py
@@ -54,13 +54,15 @@
     nx, ny = lax.axis_size("gx"), lax.axis_size("gy")
     z = lax.rem(gy, PLANES)
     even, first = lax.rem(gx, 2) == 0, gy == 0
+    start = (gx == 0) & first
     late = (
-        (z == 0) | (z == PLANES - 1),
-        z >= 2,
-        even & (((gx > 0) & (gx <= nx // 2)) | ((gx == 0) & first)),
+        (z == PLANES - 1) | start,
+        (z >= 1) & jnp.logical_not((gx == 0) & (gy == 1)),
+        even & (((gx > 0) & (gx <= nx // 2)) | start),
         even | ((gx > nx // 2) & ((gx < nx - 1) | (gy > 0))),
     )
     early = tuple(jnp.logical_not(x) for x in late)
+    beside_west, beside_east = first & (gx == 1), first & (gx == nx - 1)
     west, east = (lax.rem(gx + nx - 1, nx), gy), (lax.rem(gx + 1, nx), gy)
     south, north = (gx, lax.rem(gy + ny - 1, ny)), (gx, lax.rem(gy + 1, ny))
     neighbours = (north, south, west, east)
@@ -180,8 +182,9 @@
         for p in range(1, 128 // GROWS):
             some_gpoints(q, p, False)
         if q == 0:
-            pl.when(gy > 0)(functools.partial(each, early, answer, (2, 3)))
-            pl.when(z >= 2)(functools.partial(each, early, answer, (0, 1)))
+            pl.when(jnp.logical_not(beside_west))(functools.partial(each, early, answer, (2,)))
+            pl.when(jnp.logical_not(beside_east))(functools.partial(each, early, answer, (3,)))
+            each(early, answer, (0,))
         for t in range(GROUP):
             tile = q * GROUP + t
             parts = []
@@ -206,7 +209,8 @@
         out = pltpu.make_async_copy(heat_v.at[span], heat_out.at[span], out_sem.at[q])
         out.start()
         outs.append(out)
-    pl.when(gy == 0)(functools.partial(each, early, answer, (2, 3)))
+    pl.when(beside_west)(functools.partial(each, early, answer, (2,)))
+    pl.when(beside_east)(functools.partial(each, early, answer, (3,)))
     receive(2)
     receive(3)
     after_v[0] += 0.2 * grid[0]
@@ -214,7 +218,7 @@
     out = pltpu.make_async_copy(after_v, after_out, out_sem.at[TILES // GROUP])
     out.start()
     outs.append(out)
-    pl.when(z < 2)(functools.partial(each, early, answer, (0, 1)))
+    each(early, answer, (1,))
     receive(0)
     receive(1)
     for i in range(4):

time: 24.8 us -> 24.5 us (0.988)
  the two profiles are of different devices: /device:TPU:97 before, /device:TPU:112 now
where the time goes in v5:
time: 24.5 us; the launch traced here: 24 us
  Pallas kernels  22.7 us (93%)
  between operations  1.29 us (5%)
    pallas_call x1, Pallas kernels, local(): pl.pallas_call(kernel, out_shape=tuple((jax.ShapeDtypeStruct(x, F32) for...  20.7 us
    pallas_call x1, Pallas kernels, local(): pl.pallas_call(finish, out_shape=tuple((jax.ShapeDtypeStruct(block, F32)...  2.04 us

profile of v5, /device:TPU:112, one launch (start us, length us, event | category | flops | bytes accessed | tf_op | source)
XLA Modules:
  0.0 24.0 jit_solution(5126109415212406936)
XLA Ops:
  1.3 20.7 %shard_map.95 = (f32[16,64,128]{2,1,0:T(8,128)}, f32[16,64,128]{2,1,0:T(8,128)}, f32[16,128]{1,0:T(8,128)}, f32[16,128]{1,0:T(8,128)}) custom-call(f32[16,64,128]{2,1,0:T(8,128)} %kelvin.1, f32[16,64,128]{2,1,0:T(8,128)} %vapour.1, s32[16,64]{1,0:T(8,128)} %cloud.1, bf16[16,64]{1,0:T(8,128)(2,1)} %cosine.1, s32[1,1024]{1,0:T(1,128)} %bitcast.2, ...), custom_call_target="tpu_custom_call" | custom-call | flops 67108864 | bytes 2097152 | tf_op jit(solution)/shard_map/pallas_call | solution.py:261
  22.0 2.0 %shard_map.96 = (f32[16,64,128]{2,1,0:T(8,128)}, f32[16,64,128]{2,1,0:T(8,128)}) custom-call(f32[16,64,128]{2,1,0:T(8,128)} %get-tuple-element.6.after, f32[16,64,128]{2,1,0:T(8,128)} %get-tuple-element.7.heat, f32[16,128]{1,0:T(8,128)} %get-tuple-element.8.south, f32[16,128]{1,0:T(8,128)} %get-tuple-element.9.north), custom_call_target="tpu_custom_call" | custom-call | tf_op jit(solution)/shard_map/pallas_call | solution.py:303

commit v6 on v5

--- a/solution.py
+++ b/solution.py
@@ -69,17 +69,22 @@
     mine = (kelvin.at[:, CY - 1], kelvin.at[:, 0], kelvin.at[0], kelvin.at[CX - 1])
     lands = (south_out, north_out, grid.at[CX + 1], grid.at[0])
     back = (1, 0, 3, 2)
-    sends = [
-        pltpu.make_async_remote_copy(
-            src_ref=mine[i],
-            dst_ref=lands[i],
-            send_sem=send_sem.at[i],
-            recv_sem=recv_sem.at[i],
-            device_id=neighbours[i],
-            device_id_type=MESH,
-        )
-        for i in range(4)
-    ]
+    inside = grid.at[pl.ds(1, CX)]
+    loaded = (inside.at[:, CY - 1], inside.at[:, 0], inside.at[0], inside.at[CX - 1])
+    sends, answers = (
+        [
+            pltpu.make_async_remote_copy(
+                src_ref=edges[i],
+                dst_ref=lands[i],
+                send_sem=send_sem.at[i],
+                recv_sem=recv_sem.at[i],
+                device_id=neighbours[i],
+                device_id_type=MESH,
+            )
+            for i in range(4)
+        ]
+        for edges in (mine, loaded)
+    )
     barrier = pltpu.get_barrier_semaphore()
 
     def greet(i):
@@ -95,7 +100,7 @@
 
     def answer(i):
         pl.semaphore_wait(here_sem.at[i], 1)
-        sends[i].start()
+        answers[i].start()
 
     def receive(i):
         sends[back[i]].wait_recv()

time: 24.5 us -> 24.5 us (level)
  no operation moved by 1% of the time
where the time goes in v6:
time: 24.5 us; the launch traced here: 24 us
  Pallas kernels  22.7 us (93%)
  between operations  1.29 us (5%)
    pallas_call x1, Pallas kernels, local(): pl.pallas_call(kernel, out_shape=tuple((jax.ShapeDtypeStruct(x, F32) for...  20.7 us
    pallas_call x1, Pallas kernels, local(): pl.pallas_call(finish, out_shape=tuple((jax.ShapeDtypeStruct(block, F32)...  2.04 us

profile of v6, /device:TPU:112, one launch (start us, length us, event | category | flops | bytes accessed | tf_op | source)
XLA Modules:
  0.0 24.0 jit_solution(9018416252053496374)
XLA Ops:
  1.3 20.7 %shard_map.95 = (f32[16,64,128]{2,1,0:T(8,128)}, f32[16,64,128]{2,1,0:T(8,128)}, f32[16,128]{1,0:T(8,128)}, f32[16,128]{1,0:T(8,128)}) custom-call(f32[16,64,128]{2,1,0:T(8,128)} %kelvin.1, f32[16,64,128]{2,1,0:T(8,128)} %vapour.1, s32[16,64]{1,0:T(8,128)} %cloud.1, bf16[16,64]{1,0:T(8,128)(2,1)} %cosine.1, s32[1,1024]{1,0:T(1,128)} %bitcast.2, ...), custom_call_target="tpu_custom_call" | custom-call | flops 67108864 | bytes 2097152 | tf_op jit(solution)/shard_map/pallas_call | solution.py:266
  22.0 2.0 %shard_map.96 = (f32[16,64,128]{2,1,0:T(8,128)}, f32[16,64,128]{2,1,0:T(8,128)}) custom-call(f32[16,64,128]{2,1,0:T(8,128)} %get-tuple-element.6.after, f32[16,64,128]{2,1,0:T(8,128)} %get-tuple-element.7.heat, f32[16,128]{1,0:T(8,128)} %get-tuple-element.8.south, f32[16,128]{1,0:T(8,128)} %get-tuple-element.9.north), custom_call_target="tpu_custom_call" | custom-call | tf_op jit(solution)/shard_map/pallas_call | solution.py:308
